TPU v7x, 32 devices: a whole 2x2x4 slice. The times are simulated.
32 devices in a mesh: cls: 2 (over y), pts: 4 (over z), sub: 2 (over x), rep: 2 (over core).
Axes of the slice: x: 2, y: 2, z: 4, core: 2. Of those that a mesh axis runs over, the one named last changes fastest.
Arguments:
- right_sides: bfloat16 [128, 131072], P('rep', ('cls', 'pts', 'sub')), parts along dimension 1, may hold values from -6 to 6
- curve_order: int32 [16, 8192], P(('cls', 'pts', 'sub')), parts along dimension 0, may hold values from 0 to 8191, each once within a row
- level_bases: bfloat16 [4, 128, 131072], P(None, 'rep', ('cls', 'pts', 'sub')), parts along dimension 2, may hold values from -0.0234375 to 0.0234375
- capacitance: float32 [30, 256, 256], P('cls'), parts along dimension 0
Outputs:
- solved: bfloat16 [128, 131072], P('rep', ('cls', 'pts', 'sub')), parts along dimension 1
There are 2 independent parts, one for each index of `cls`. A program takes and returns all parts, laid end to end along the dimension named above; each array names one. Nothing has to cross between parts.
All inputs are finite; a program needn't handle non-finite values.
Results may differ from a plain program's by a relative error of at most 0.014.
Values may be sent and summed in bfloat16 or wider, within the bound.
A program may use at most 64 MiB of HBM per device.

v0:
```python
import math

import jax
import jax.numpy as jnp
from jax import lax
from jax.sharding import PartitionSpec as P

RANK = 128
LEVELS = 4


def from_partner(array, axis, stride):
    return lax.ppermute(array, axis, [(i, i ^ 1 << stride) for i in range(lax.axis_size(axis))])


def shards(right_sides, curve_order, level_bases, capacitance):
    block_total = lax.axis_size(("pts", "sub"))
    my_block = lax.axis_index(("pts", "sub"))
    rhs_rows, point_count = right_sides.shape
    rank_width = capacitance.shape[1] // 2
    total_points = point_count * block_total
    current = jnp.take(right_sides, curve_order[0], axis=0 + 1).astype(jnp.float32)
    for tree_level in range(LEVELS, 0, -1):
        node_count = 2**tree_level
        node_size = total_points // node_count
        span_devices = max(node_size // point_count, 1)
        local_nodes = max(point_count // node_size, 1)
        node_width = point_count // local_nodes
        level_basis = lax.all_gather(level_bases[tree_level - 1], "rep", axis=0, tiled=True)
        level_basis = level_basis.reshape(rank_width, local_nodes, node_width)
        rounded = current.astype(jnp.bfloat16).reshape(rhs_rows, local_nodes, node_width)
        partial_value = jnp.einsum(
            "rmw,kmw->mrk", rounded, level_basis, preferred_element_type=jnp.float32
        )
        first_node = my_block // span_devices * local_nodes
        odd_child = first_node % 2 == 1
        if local_nodes >= 2:
            child_pairs = partial_value.reshape(local_nodes // 2, 2, rhs_rows, rank_width)
            stacked = jnp.concatenate([child_pairs[:, 0], child_pairs[:, 1]], axis=2)
        else:
            summed = partial_value[0]
            for bit_index in range(span_devices.bit_length() - 1):
                summed = summed + from_partner(
                    summed.astype(jnp.bfloat16), ("pts", "sub"), bit_index
                ).astype(summed.dtype)
            sibling_sum = from_partner(
                summed.astype(jnp.bfloat16), ("pts", "sub"), span_devices.bit_length() - 1
            ).astype(summed.dtype)
            left_sum = jnp.where(odd_child, sibling_sum, summed)
            right_sum = jnp.where(odd_child, summed, sibling_sum)
            stacked = jnp.concatenate([left_sum, right_sum], axis=1)[None]
        parent_local = max(local_nodes // 2, 1)
        parent = node_count // 2 - 1 + first_node // 2
        cap_blocks = lax.dynamic_slice_in_dim(capacitance, parent, parent_local, 0)
        factor = 0.3 * node_count * math.sqrt(node_size / RANK)
        coefficients = (
            jnp.einsum("prb,pab->pra", stacked, cap_blocks, precision=lax.Precision.HIGHEST)
            * factor
        )
        if local_nodes >= 2:
            coefficients = (
                coefficients.reshape(parent_local, rhs_rows, 2, rank_width)
                .transpose(0, 2, 1, 3)
                .reshape(local_nodes, rhs_rows, rank_width)
            )
        else:
            coefficients = jnp.where(
                odd_child, coefficients[0, :, rank_width:], coefficients[0, :, :rank_width]
            )[None]
        coefficients = coefficients.astype(jnp.bfloat16)
        update = jnp.einsum(
            "mrk,kmw->rmw", coefficients, level_basis, preferred_element_type=jnp.float32
        )
        current = current - update.reshape(rhs_rows, point_count)
    return current.astype(jnp.bfloat16)


def solution(mesh):
    in_specs = (
        P("rep", ("cls", "pts", "sub")),
        P(("cls", "pts", "sub"), None),
        P(None, "rep", ("cls", "pts", "sub")),
        P("cls", None, None),
    )
    out_specs = P("rep", ("cls", "pts", "sub"))
    return jax.shard_map(shards, mesh=mesh, in_specs=in_specs, out_specs=out_specs, check_vma=False)
```

profile of v0, /device:TPU:0, one launch (start us, length us, event | category | flops | bytes accessed | tf_op | source)
XLA Modules:
  0.0 117.7 jit_solution(8034529759324220718)
XLA Ops:
  6.5 4.3 %fusion.69 = (bf16[1,64,8192]{2,1,0:T(8,128)(2,1)}, bf16[1,64,8192]{2,1,0:T(8,128)(2,1)}, bf16[1,64,8192]{2,1,0:T(8,128)(2,1)}, bf16[1,64,8192]{2,1,0:T(8,128)(2,1)}) fusion(bf16[4,64,8192]{2,1,0:T(8,128)(2,1)} %param.6), kind=kLoop, calls=%fused_computation.100 | loop fusion | bytes 8388608 | tf_op jit(solution)/shard_map/slice | solution.py:29
  10.9 0.7 all-gather.11.cloned.1.call-update
  11.6 0.7 all-gather.13.cloned.1.call-update
  12.9 1.1 copy.16
  14.1 29.2 %gather_fusion = bf16[8192,64]{1,0:T(8,128)(2,1)} fusion(bf16[64,8192]{0,1:T(8,128)(2,1)S(1)} %copy.16, s32[8192]{0:T(1024)S(1)} %broadcast_clamp_fusion), kind=kCustom, calls=%fused_computation | custom fusion | bytes 2129920 | tf_op jit(solution)/shard_map/jit(_take)/gather | solution.py:22
  43.3 1.9 %copy.17 = bf16[8192,64]{0,1:T(8,128)(2,1)S(1)} copy(bf16[8192,64]{1,0:T(8,128)(2,1)} %gather_fusion) | data formatting | bytes 2097152 | tf_op jit(solution)/shard_map/jit(_take)/gather | solution.py:22
  45.2 0.6 broadcast.88
  45.8 0.8 reduce.3
  46.7 3.4 %copy.19 = bf16[1,128,8192]{1,2,0:T(8,128)(2,1)S(1)} copy(bf16[1,128,8192]{2,1,0:T(8,128)(2,1)} %all-gather.9.cloned.1.call-done) | data formatting | bytes 4194304 | tf_op jit(solution)/shard_map/all_gather | solution.py:29
  50.7 1.4 %fusion.17 = bf16[1,64,256]{2,1,0:T(8,128)(2,1)S(1)} fusion(f32[15,256,256]{2,1,0:T(8,128)} %param.7, s32[]{:T(128)S(6)} %select_n.145, f32[1,64,128]{2,1,0:T(8,128)S(1)} %get-tuple-element.14, f32[1,64,128]{2,1,0:T(8,128)S(1)} %get-tuple-element.13), kind=kOutput, calls=%fused_computation.27 | convolution fusion | flops 50380800 | bytes 360452 | tf_op jit(solution)/shard_map/prb,pab->pra/dot_general | solution.py:57
  52.2 2.4 %fusion.74 = f32[2,64,4096]{2,1,0:T(8,128)S(1)} fusion(bf16[2,64,128]{2,1,0:T(8,128)(2,1)S(1)} %bitcast.149, bf16[128,2,4096]{0,2,1:T(8,128)(2,1)} %bitcast.145), kind=kOutput, calls=%fused_computation.105 | convolution fusion | flops 134217728 | bytes 4227072 | tf_op jit(solution)/shard_map/mrk,kmw->rmw/dot_general | solution.py:71
  54.9 1.0 copy.29
  55.9 2.8 %fusion.71 = (bf16[64,128]{1,0:T(8,128)(2,1)S(1)}, f32[64,128]{1,0:T(8,128)S(1)}) fusion(bf16[64,8192]{1,0:T(8,128)(2,1)} %bitcast.147, bf16[1,128,8192]{2,1,0:T(8,128)(2,1)} %all-gather.11.cloned.1.call-done), kind=kOutput, calls=%fused_computation.102 | convolution fusion | flops 134225920 | bytes 3194880 | tf_op jit(solution)/shard_map/rmw,kmw->mrk/dot_general | solution.py:32
  58.7 2.8 %collective-permute-start = (bf16[64,128]{1,0:T(8,128)(2,1)S(1)}, bf16[64,128]{1,0:T(8,128)(2,1)S(1)}, u32[]{:S(2)}, u32[]{:S(2)}) collective-permute-start(bf16[64,128]{1,0:T(8,128)(2,1)S(1)} %get-tuple-element.19), channel_id=1, source_target_pairs={{0,2},{2,0},{4,6},{6,4},{8,10},{10,8},{12,14},{14,12},{1,3},{3,1},... | collective-permute-start | bytes 49160 | tf_op jit(solution)/shard_map/ppermute | solution.py:13
  61.6 3.0 %copy.22 = f32[64,2,4096]{2,1,0:T(2,128)} copy(f32[64,2,4096]{2,0,1:T(8,128)S(1)} %bitcast.140) | data formatting | bytes 4194304 | tf_op jit(solution)/shard_map/mrk,kmw->rmw/transpose | solution.py:71
  64.6 4.1 %reshape.198 = f32[64,1,8192]{2,0,1:T(8,128)} reshape(f32[64,2,4096]{2,1,0:T(2,128)} %copy.22) | data formatting | bytes 4194304 | tf_op jit(solution)/shard_map/reshape | solution.py:74
  68.7 1.3 %fusion.15 = bf16[1,64,256]{2,1,0:T(8,128)(2,1)S(1)} fusion(f32[15,256,256]{2,1,0:T(8,128)} %param.7, s32[]{:T(128)S(6)} %select_n.152, f32[64,128]{1,0:T(8,128)S(1)} %get-tuple-element.16, f32[64,128]{1,0:T(8,128)S(1)} %get-tuple-element.15), kind=kOutput, calls=%fused_computation.24 | convolution fusion | flops 50380800 | bytes 360452 | tf_op jit(solution)/shard_map/prb,pab->pra/dot_general | solution.py:57
  70.1 3.4 %fusion.9 = f32[64,8192]{1,0:T(8,128)} fusion(bf16[1,128,8192]{2,1,0:T(8,128)(2,1)} %all-gather.11.cloned.1.call-done, bf16[1,64,256]{2,1,0:T(8,128)(2,1)S(1)} %fusion.15, pred[]{:T(512)S(6)} %eq.13), kind=kOutput, calls=%fused_computation.13 | convolution fusion | flops 134225920 | bytes 4227073 | tf_op jit(solution)/shard_map/mrk,kmw->rmw/dot_general | solution.py:71
  73.5 3.7 %fusion.72 = (bf16[64,128]{1,0:T(8,128)(2,1)S(1)}, f32[64,128]{1,0:T(8,128)S(1)}) fusion(bf16[1,128,8192]{2,1,0:T(8,128)(2,1)} %all-gather.13.cloned.1.call-done, f32[64,8192]{1,0:T(8,128)} %fusion.9, f32[64,1,8192]{2,0,1:T(8,128)} %reshape.198, bf16[8192,64]{0,1:T(8,128)(2,1)S(1)} %copy.17, pred[8192]{0:T(1024)(128)(4,1)S(1)} %compare_and_fusion.1), kind=kOutput, calls=%fused_computation.103 | convolution fusion | flops 136847360 | bytes 7397376 | tf_op jit(solution)/shard_map/rmw,kmw->mrk/dot_general | solution.py:32
  77.2 3.7 %collective-permute-done.1 = bf16[64,128]{1,0:T(8,128)(2,1)S(1)} collective-permute-done((bf16[64,128]{1,0:T(8,128)(2,1)S(1)}, bf16[64,128]{1,0:T(8,128)(2,1)S(1)}, u32[]{:S(2)}, u32[]{:S(2)}) %collective-permute-start.1) | collective-permute-done | bytes 16416 | tf_op jit(solution)/shard_map/ppermute | solution.py:13
  81.0 1.6 %collective-permute-start.2 = (bf16[64,128]{1,0:T(8,128)(2,1)S(1)}, bf16[64,128]{1,0:T(8,128)(2,1)S(1)}, u32[]{:S(2)}, u32[]{:S(2)}) collective-permute-start(bf16[64,128]{1,0:T(8,128)(2,1)S(1)} %fusion.56), channel_id=1, source_target_pairs={{0,4},{2,6},{4,0},{6,2},{8,12},{10,14},{12,8},{14,10},{1,5},{3,7},... | collective-permute-start | bytes 49160 | tf_op jit(solution)/shard_map/ppermute | solution.py:13
  82.6 2.2 %collective-permute-done.2 = bf16[64,128]{1,0:T(8,128)(2,1)S(1)} collective-permute-done((bf16[64,128]{1,0:T(8,128)(2,1)S(1)}, bf16[64,128]{1,0:T(8,128)(2,1)S(1)}, u32[]{:S(2)}, u32[]{:S(2)}) %collective-permute-start.2) | collective-permute-done | bytes 16416 | tf_op jit(solution)/shard_map/ppermute | solution.py:13
  84.8 1.3 %fusion.14 = bf16[1,64,256]{2,1,0:T(8,128)(2,1)S(1)} fusion(f32[15,256,256]{2,1,0:T(8,128)} %param.7, s32[]{:T(128)S(6)} %select_n.161, f32[64,128]{1,0:T(8,128)S(1)} %get-tuple-element.12, f32[64,128]{1,0:T(8,128)S(1)} %get-tuple-element.11), kind=kOutput, calls=%fused_computation.22 | convolution fusion | flops 50380800 | bytes 360452 | tf_op jit(solution)/shard_map/prb,pab->pra/dot_general | solution.py:57
  86.1 3.4 %fusion.5 = f32[64,8192]{1,0:T(8,128)} fusion(bf16[1,128,8192]{2,1,0:T(8,128)(2,1)} %all-gather.13.cloned.1.call-done, bf16[1,64,256]{2,1,0:T(8,128)(2,1)S(1)} %fusion.14, pred[]{:T(512)S(6)} %eq.14), kind=kOutput, calls=%fused_computation.9 | convolution fusion | flops 134225920 | bytes 4227073 | tf_op jit(solution)/shard_map/mrk,kmw->rmw/dot_general | solution.py:71
  89.5 4.4 %fusion.73 = (bf16[64,128]{1,0:T(8,128)(2,1)S(1)}, f32[64,128]{1,0:T(8,128)S(1)}) fusion(bf16[1,128,8192]{2,1,0:T(8,128)(2,1)} %all-gather.15.cloned.1.call-done, f32[64,8192]{1,0:T(8,128)} %fusion.5, f32[64,8192]{1,0:T(8,128)} %fusion.9, f32[64,1,8192]{2,0,1:T(8,128)} %reshape.198, bf16[8192,64]{0,1:T(8,128)(2,1)S(1)} %copy.17, ...), kind=kOutput, calls=%fused_computation.104 | convolution fusion | flops 137371648 | bytes 9494528 | tf_op jit(solution)/shard_map/rmw,kmw->mrk/dot_general | solution.py:32
  94.1 3.6 %collective-permute-done.3 = bf16[64,128]{1,0:T(8,128)(2,1)S(1)} collective-permute-done((bf16[64,128]{1,0:T(8,128)(2,1)S(1)}, bf16[64,128]{1,0:T(8,128)(2,1)S(1)}, u32[]{:S(2)}, u32[]{:S(2)}) %collective-permute-start.3) | collective-permute-done | bytes 16416 | tf_op jit(solution)/shard_map/ppermute | solution.py:13
  97.7 1.6 %collective-permute-start.4 = (bf16[64,128]{1,0:T(8,128)(2,1)S(1)}, bf16[64,128]{1,0:T(8,128)(2,1)S(1)}, u32[]{:S(2)}, u32[]{:S(2)}) collective-permute-start(bf16[64,128]{1,0:T(8,128)(2,1)S(1)} %fusion.46), channel_id=1, source_target_pairs={{0,4},{2,6},{4,0},{6,2},{8,12},{10,14},{12,8},{14,10},{1,5},{3,7},... | collective-permute-start | bytes 49160 | tf_op jit(solution)/shard_map/ppermute | solution.py:13
  99.3 2.2 %collective-permute-done.4 = bf16[64,128]{1,0:T(8,128)(2,1)S(1)} collective-permute-done((bf16[64,128]{1,0:T(8,128)(2,1)S(1)}, bf16[64,128]{1,0:T(8,128)(2,1)S(1)}, u32[]{:S(2)}, u32[]{:S(2)}) %collective-permute-start.4) | collective-permute-done | bytes 16416 | tf_op jit(solution)/shard_map/ppermute | solution.py:13
  101.5 2.7 %collective-permute-start.5 = (bf16[64,128]{1,0:T(8,128)(2,1)S(1)}, bf16[64,128]{1,0:T(8,128)(2,1)S(1)}, u32[]{:S(2)}, u32[]{:S(2)}) collective-permute-start(bf16[64,128]{1,0:T(8,128)(2,1)S(1)} %fusion.68), channel_id=1, source_target_pairs={{0,8},{2,10},{4,12},{6,14},{8,0},{10,2},{12,4},{14,6},{1,9},{3,11}... | collective-permute-start | bytes 49160 | tf_op jit(solution)/shard_map/ppermute | solution.py:13
  104.4 1.9 %collective-permute-done.5 = bf16[64,128]{1,0:T(8,128)(2,1)S(1)} collective-permute-done((bf16[64,128]{1,0:T(8,128)(2,1)S(1)}, bf16[64,128]{1,0:T(8,128)(2,1)S(1)}, u32[]{:S(2)}, u32[]{:S(2)}) %collective-permute-start.5) | collective-permute-done | bytes 16416 | tf_op jit(solution)/shard_map/ppermute | solution.py:13
  106.2 1.3 %fusion.13 = bf16[1,64,256]{2,1,0:T(8,128)(2,1)S(1)} fusion(f32[15,256,256]{2,1,0:T(8,128)} %param.7, s32[]{:T(128)S(6)} %select_n.170, f32[64,128]{1,0:T(8,128)S(1)} %get-tuple-element.10, f32[64,128]{1,0:T(8,128)S(1)} %get-tuple-element.9), kind=kOutput, calls=%fused_computation.20 | convolution fusion | flops 50380800 | bytes 360452 | tf_op jit(solution)/shard_map/prb,pab->pra/dot_general | solution.py:57
  107.6 3.6 %fusion = bf16[64,8192]{1,0:T(8,128)(2,1)} fusion(bf16[1,128,8192]{2,1,0:T(8,128)(2,1)} %all-gather.15.cloned.1.call-done, f32[64,8192]{1,0:T(8,128)S(1)} %copy-done.1, f32[64,8192]{1,0:T(8,128)S(1)} %copy-done, f32[64,8192]{1,0:T(8,128)S(1)} %bitcast.146, bf16[8192,64]{0,1:T(8,128)(2,1)S(1)} %copy.17, pred[8192]{0:T(1024)(128)(4,1)S(1)} %compare_and_fusion.1, ...), kind=kOutput, calls=%fused_computation.2 | convolution fusion | flops 137895936 | bytes 10526721 | tf_op jit(solution)/shard_map/mrk,kmw->rmw/dot_general | solution.py:71
  (40 shorter events, 2.1 us)
Async XLA Ops:
  6.5 40.1 %all-gather.9.cloned.1.call-start = ((), (), s32[]{:S(2)}) async-start(), calls=%async_computation | async-start | bytes 3145728 | tf_op jit(solution)/shard_map/all_gather | solution.py:29
  10.8 2.1 %copy-start.3 = (bf16[64,8192]{1,0:T(8,128)(2,1)S(1)}, bf16[64,8192]{1,0:T(8,128)(2,1)}, u32[]{:S(2)}) copy-start(bf16[64,8192]{1,0:T(8,128)(2,1)} %param.4) | copy-start | bytes 3145732
  10.8 45.1 %all-gather.11.cloned.1.call-start = ((), (), s32[]{:S(2)}) async-start(), calls=%async_computation.1 | async-start | bytes 3145728 | tf_op jit(solution)/shard_map/all_gather | solution.py:29
  11.6 61.9 %all-gather.13.cloned.1.call-start = ((), (), s32[]{:S(2)}) async-start(), calls=%async_computation.2 | async-start | bytes 3145728 | tf_op jit(solution)/shard_map/all_gather | solution.py:29
  12.3 77.2 %all-gather.15.cloned.1.call-start = ((), (), s32[]{:S(2)}) async-start(), calls=%async_computation.3 | async-start | bytes 3145728 | tf_op jit(solution)/shard_map/all_gather | solution.py:29
  12.4 1.6 %copy-start.4 = (s32[1,8192]{1,0:T(1,128)S(1)}, s32[1,8192]{1,0:T(1,128)}, u32[]{:S(2)}) copy-start(s32[1,8192]{1,0:T(1,128)} %param.5) | copy-start | bytes 98308
  50.1 2.0 %copy-start.2 = (bf16[1,128,8192]{1,2,0:T(8,128)(2,1)}, bf16[1,128,8192]{1,2,0:T(8,128)(2,1)S(1)}, u32[]{:S(2)}) copy-start(bf16[1,128,8192]{1,2,0:T(8,128)(2,1)S(1)} %copy.19) | copy-start | bytes 6291460
  58.7 10.0 %collective-permute-start = (bf16[64,128]{1,0:T(8,128)(2,1)S(1)}, bf16[64,128]{1,0:T(8,128)(2,1)S(1)}, u32[]{:S(2)}, u32[]{:S(2)}) collective-permute-start(bf16[64,128]{1,0:T(8,128)(2,1)S(1)} %get-tuple-element.19), channel_id=1, source_target_pairs={{0,2},{2,0},{4,6},{6,4},{8,10},{10,8},{12,14},{14,12},{1,3},{3,1},... | collective-permute-start | bytes 49160 | tf_op jit(solution)/shard_map/ppermute | solution.py:13
  77.2 3.8 %collective-permute-start.1 = (bf16[64,128]{1,0:T(8,128)(2,1)S(1)}, bf16[64,128]{1,0:T(8,128)(2,1)S(1)}, u32[]{:S(2)}, u32[]{:S(2)}) collective-permute-start(bf16[64,128]{1,0:T(8,128)(2,1)S(1)} %get-tuple-element.21), channel_id=1, source_target_pairs={{0,2},{2,0},{4,6},{6,4},{8,10},{10,8},{12,14},{14,12},{1,3},{3,1},... | collective-permute-start | bytes 49160 | tf_op jit(solution)/shard_map/ppermute | solution.py:13
  81.0 3.8 %collective-permute-start.2 = (bf16[64,128]{1,0:T(8,128)(2,1)S(1)}, bf16[64,128]{1,0:T(8,128)(2,1)S(1)}, u32[]{:S(2)}, u32[]{:S(2)}) collective-permute-start(bf16[64,128]{1,0:T(8,128)(2,1)S(1)} %fusion.56), channel_id=1, source_target_pairs={{0,4},{2,6},{4,0},{6,2},{8,12},{10,14},{12,8},{14,10},{1,5},{3,7},... | collective-permute-start | bytes 49160 | tf_op jit(solution)/shard_map/ppermute | solution.py:13
  93.9 3.8 %collective-permute-start.3 = (bf16[64,128]{1,0:T(8,128)(2,1)S(1)}, bf16[64,128]{1,0:T(8,128)(2,1)S(1)}, u32[]{:S(2)}, u32[]{:S(2)}) collective-permute-start(bf16[64,128]{1,0:T(8,128)(2,1)S(1)} %get-tuple-element.23), channel_id=1, source_target_pairs={{0,2},{2,0},{4,6},{6,4},{8,10},{10,8},{12,14},{14,12},{1,3},{3,1},... | collective-permute-start | bytes 49160 | tf_op jit(solution)/shard_map/ppermute | solution.py:13
  97.7 3.8 %collective-permute-start.4 = (bf16[64,128]{1,0:T(8,128)(2,1)S(1)}, bf16[64,128]{1,0:T(8,128)(2,1)S(1)}, u32[]{:S(2)}, u32[]{:S(2)}) collective-permute-start(bf16[64,128]{1,0:T(8,128)(2,1)S(1)} %fusion.46), channel_id=1, source_target_pairs={{0,4},{2,6},{4,0},{6,2},{8,12},{10,14},{12,8},{14,10},{1,5},{3,7},... | collective-permute-start | bytes 49160 | tf_op jit(solution)/shard_map/ppermute | solution.py:13
  101.5 4.7 %collective-permute-start.5 = (bf16[64,128]{1,0:T(8,128)(2,1)S(1)}, bf16[64,128]{1,0:T(8,128)(2,1)S(1)}, u32[]{:S(2)}, u32[]{:S(2)}) collective-permute-start(bf16[64,128]{1,0:T(8,128)(2,1)S(1)} %fusion.68), channel_id=1, source_target_pairs={{0,8},{2,10},{4,12},{6,14},{8,0},{10,2},{12,4},{14,6},{1,9},{3,11}... | collective-permute-start | bytes 49160 | tf_op jit(solution)/shard_map/ppermute | solution.py:13
  104.2 3.4 %copy-start = (f32[64,8192]{1,0:T(8,128)S(1)}, f32[64,8192]{1,0:T(8,128)}, u32[]{:S(2)}) copy-start(f32[64,8192]{1,0:T(8,128)} %fusion.9) | copy-start | bytes 6291460
  104.2 3.4 %copy-start.1 = (f32[64,8192]{1,0:T(8,128)S(1)}, f32[64,8192]{1,0:T(8,128)}, u32[]{:S(2)}) copy-start(f32[64,8192]{1,0:T(8,128)} %fusion.5) | copy-start | bytes 6291460
Sparse Core Ops, SparseCore 0:
  11.0 13.2 all-gather.8
  25.8 11.7 all-gather.10
  39.1 11.7 all-gather.12
  52.3 11.7 all-gather.14
where the time goes:
time: 118 us
  local copies, waits for them, and re-layouts  48.8 us (41%)
  matrix products  29.6 us (25%)
  waiting for transfers between devices  15.5 us (13%)
  between operations  13.4 us (11%)
  starting transfers between devices  9.18 us (8%)
  other arithmetic  1.2 us (1%)
    gather x2, local copies, waits for them, and re-layouts, shards(): jnp.take(right_sides, curve_order[0], axis=0 + 1).astype(jnp.float32)  31.1 us
    ppermute x6, waiting for transfers between devices, from_partner(): lax.ppermute(array, axis, [(i, i ^ 1 << stride) for i in range(lax.axis_s...  13.6 us
    dot_general x4, matrix products, shards(): jnp.einsum('mrk,kmw->rmw', coefficients, level_basis, preferred_element_t...  12.8 us
    dot_general x4, matrix products, shards(): jnp.einsum('rmw,kmw->mrk', rounded, level_basis, preferred_element_type=j...  11.4 us
    ppermute x6, starting transfers between devices, from_partner(): lax.ppermute(array, axis, [(i, i ^ 1 << stride) for i in range(lax.axis_s...  9.06 us
    dot_general x4, matrix products, shards(): jnp.einsum('prb,pab->pra', stacked, cap_blocks, precision=lax.Precision.H...  5.42 us
    slice x1, local copies, waits for them, and re-layouts, shards(): level_bases[tree_level - 1]  4.27 us
    reshape x2, local copies, waits for them, and re-layouts, shards(): current = current - update.reshape(rhs_rows, point_count)  4.26 us
  transfers between devices with their start and end apart: 10, of which 5 were waited for; matrix products, arithmetic and copies ran while one was open for 56% of the time, Pallas kernels for 0%

commit v1 on v0

v1 whole, which is shorter than its diff:
```python
import functools
import math

import jax
import jax.numpy as jnp
from jax import lax
from jax.experimental import pallas as pl
from jax.experimental.pallas import tpu as pltpu
from jax.sharding import PartitionSpec as P

RANK = 128
LEVELS = 4
LANES = 128
CHUNK = 2048
STAGE_BITS = 2
MESH = pl.DeviceIdType.MESH
F32 = jnp.float32
BF16 = jnp.bfloat16


def dot_nt(a, b):
    return lax.dot_general(a, b, (((1,), (1,)), ((), ())), preferred_element_type=F32)


def gather_kernel(order, x, out, table, rows_a, rows_b):
    rhs, points = x.shape
    blocks = points // LANES

    @pl.loop(0, blocks, unroll=4)
    def _(b):
        cols = pl.ds(pl.multiple_of(b * LANES, LANES), LANES)
        table[cols, 0:rhs] = x[:, cols].astype(F32).T

    def pick(b, rows):
        for j in range(LANES):
            rows[pl.ds(j, 1), :] = table[pl.ds(order[0, b * LANES + j], 1), :]

    def put(b, rows):
        cols = pl.ds(pl.multiple_of(b * LANES, LANES), LANES)
        out[:, cols] = rows[...].T[0:rhs].astype(BF16)

    pick(0, rows_a)

    @pl.loop(0, blocks // 2 - 1)
    def _(i):
        pick(2 * i + 1, rows_b)
        put(2 * i, rows_a)
        pick(2 * i + 2, rows_a)
        put(2 * i + 1, rows_b)

    pick(blocks - 1, rows_b)
    put(blocks - 2, rows_a)
    put(blocks - 1, rows_b)


def gather(order, x):
    rhs, points = x.shape
    return pl.pallas_call(
        gather_kernel,
        out_shape=jax.ShapeDtypeStruct((rhs, points), BF16),
        in_specs=[
            pl.BlockSpec(memory_space=pltpu.SMEM),
            pl.BlockSpec(memory_space=pltpu.VMEM),
        ],
        out_specs=pl.BlockSpec(memory_space=pltpu.VMEM),
        scratch_shapes=[
            pltpu.VMEM((points, LANES), F32),
            pltpu.VMEM((LANES, LANES), F32),
            pltpu.VMEM((LANES, LANES), F32),
        ],
        compiler_params=pltpu.CompilerParams(vmem_limit_bytes=24 * 2**20),
        cost_estimate=pl.CostEstimate(
            flops=points * LANES * 64, bytes_accessed=16 * rhs * points, transcendentals=0
        ),
        name="curve_gather",
    )(order, x)


def plan(points, total):
    levels, slot = [], 0
    for level in range(LEVELS, 0, -1):
        size = total // 2**level
        span, local = max(size // points, 1), max(points // size, 1)
        stages = []
        if local == 1:
            sibling = span.bit_length() - 1
            bits = list(range(sibling + 1))
            for at in range(0, len(bits), STAGE_BITS):
                group = bits[at : at + STAGE_BITS]
                masks = []
                for mix in range(1, 2 ** len(group)):
                    mask = sum(1 << bit for i, bit in enumerate(group) if mix >> i & 1)
                    masks.append((mask, bool(mask >> sibling & 1), slot))
                    slot += 1
                stages.append(masks)
        factor = 0.3 * 2**level * math.sqrt(size / RANK)
        levels.append((level, span, local, stages, factor))
    return levels, slot


def split(value):
    high = value.astype(BF16)
    return high, (value - high.astype(F32)).astype(BF16)


def solve_kernel(
    levels, x, own, other, cap, out, current, basis, caps, send, recv,
    basis_sems, cap_sems, send_sems, recv_sems,
):
    rhs, points = x.shape
    half = own.shape[1]
    sub_size = lax.axis_size("sub")
    sub_bits = sub_size.bit_length() - 1
    pts, sub = lax.axis_index("pts"), lax.axis_index("sub")
    rep = lax.axis_index("rep")
    block = pts * sub_size + sub

    def partner(mask):
        def flip(value, bits):
            for i in range(bits.bit_length()):
                if bits >> i & 1:
                    value = value + (1 << i) * (1 - 2 * (value // (1 << i) % 2))
            return value

        return {"pts": flip(pts, mask >> sub_bits), "sub": flip(sub, mask & sub_size - 1)}

    masks = sorted({m for _, _, _, stages, _ in levels for stage in stages for m, _, _ in stage})
    barrier = pltpu.get_barrier_semaphore()
    for mask in masks:
        pl.semaphore_signal(barrier, inc=1, device_id=partner(mask), device_id_type=MESH)

    basis_copies, cap_copies = [], []
    for n, (level, span, local, _, _) in enumerate(levels):
        first = block // span * local
        parent = 2 ** (level - 1) - 1 + first // 2
        odd = first % 2
        copies = []
        for piece, source in enumerate((own, other)):
            row = rep * half if piece == 0 else (1 - rep) * half
            copies.append(
                pltpu.make_async_copy(
                    source.at[level - 1],
                    basis.at[n, pl.ds(pl.multiple_of(row, half), half), :],
                    basis_sems.at[n, piece],
                )
            )
        basis_copies.append(copies)
        if local == 1:
            mine = pl.ds(pl.multiple_of(odd * RANK, RANK), RANK)
            theirs = pl.ds(pl.multiple_of((1 - odd) * RANK, RANK), RANK)
            cap_copies.append(
                [
                    pltpu.make_async_copy(
                        cap.at[parent, mine, cols],
                        caps.at[n, 0:RANK, piece * RANK : (piece + 1) * RANK],
                        cap_sems.at[n, piece],
                    )
                    for piece, cols in enumerate((mine, theirs))
                ]
            )
        else:
            cap_copies.append([pltpu.make_async_copy(cap.at[parent], caps.at[n], cap_sems.at[n, 0])])
        for copy in copies + cap_copies[-1]:
            copy.start()

    def chunk(i):
        return pl.ds(pl.multiple_of(i * CHUNK, CHUNK), CHUNK)

    steps = points // CHUNK

    def wait_basis(n):
        for copy in basis_copies[n]:
            copy.wait()

    wait_basis(0)
    local = levels[0][2]
    per_node = steps // local
    sums = []
    for node in range(local):
        def first_step(i, total):
            return total + dot_nt(x[:, chunk(i)], basis[0, :, chunk(i)])

        sums.append(
            lax.fori_loop(
                node * per_node, (node + 1) * per_node, first_step, jnp.zeros((rhs, RANK), F32)
            )
        )

    barrier_waited = False
    for n, (level, span, local, stages, factor) in enumerate(levels):
        for copy in cap_copies[n]:
            copy.wait()
        if local > 1:
            s = jnp.concatenate(sums, axis=1)
            c = caps[n]
        else:
            total = sums[0]
            sibling = None
            c = caps[n, 0:RANK, :]
            for stage in stages:
                if not barrier_waited:
                    pl.semaphore_wait(barrier, len(masks))
                    barrier_waited = True
                slot0 = stage[0][2]
                send[slot0] = total.astype(BF16)
                copies = []
                for mask, crosses, slot in stage:
                    copy = pltpu.make_async_remote_copy(
                        src_ref=send.at[slot0],
                        dst_ref=recv.at[slot],
                        send_sem=send_sems.at[slot],
                        recv_sem=recv_sems.at[slot],
                        device_id=partner(mask),
                        device_id_type=MESH,
                    )
                    copy.start()
                    copies.append(copy)
                for copy, (mask, crosses, slot) in zip(copies, stage):
                    copy.wait()
                    value = recv[slot].astype(F32)
                    if crosses:
                        sibling = value if sibling is None else sibling + value
                    else:
                        total = total + value
            s = jnp.concatenate([total, sibling], axis=1)
        c_high, c_low = split(c)
        s_high, s_low = split(s)
        coefficients = dot_nt(s_high, c_high) + dot_nt(s_low, c_high) + dot_nt(s_high, c_low)
        coefficients = (coefficients * factor).astype(BF16)
        before = x if n == 0 else current
        last = n == LEVELS - 1
        if not last:
            wait_basis(n + 1)
            next_local = levels[n + 1][2]
        pieces = max(local, 1 if last else next_local)
        width = steps // pieces
        sums = []
        for piece in range(pieces):
            node = piece * local // pieces
            mine = coefficients[:, node * RANK : (node + 1) * RANK]

            def step(i, total):
                here = chunk(i)
                update = jnp.dot(mine, basis[n, :, here], preferred_element_type=F32)
                value = before[:, here].astype(F32) - update
                if last:
                    out[:, here] = value.astype(BF16)
                    return total
                current[:, here] = value
                return total + dot_nt(value.astype(BF16), basis[n + 1, :, here])

            total = lax.fori_loop(
                piece * width, (piece + 1) * width, step, jnp.zeros((rhs, RANK), F32)
            )
            sums.append(total)
        if not last:
            group = pieces // next_local
            sums = [sum(sums[i * group + 1 : (i + 1) * group], sums[i * group]) for i in range(next_local)]


def shards(right_sides, curve_order, level_bases, capacitance):
    rhs, points = right_sides.shape
    total = points * lax.axis_size(("pts", "sub"))
    levels, slots = plan(points, total)
    other = lax.ppermute(level_bases, "rep", [(0, 1), (1, 0)])
    permuted = gather(curve_order, right_sides)
    hbm = pl.BlockSpec(memory_space=pl.ANY)
    vmem = pl.BlockSpec(memory_space=pltpu.VMEM)
    return pl.pallas_call(
        functools.partial(solve_kernel, levels),
        out_shape=jax.ShapeDtypeStruct((rhs, points), BF16),
        in_specs=[vmem, hbm, hbm, hbm],
        out_specs=vmem,
        scratch_shapes=[
            pltpu.VMEM((rhs, points), F32),
            pltpu.VMEM((LEVELS, RANK, points), BF16),
            pltpu.VMEM((LEVELS, 2 * RANK, 2 * RANK), F32),
            pltpu.VMEM((slots, rhs, RANK), BF16),
            pltpu.VMEM((slots, rhs, RANK), BF16),
            pltpu.SemaphoreType.DMA((LEVELS, 2)),
            pltpu.SemaphoreType.DMA((LEVELS, 2)),
            pltpu.SemaphoreType.DMA((slots,)),
            pltpu.SemaphoreType.DMA((slots,)),
        ],
        compiler_params=pltpu.CompilerParams(
            collective_id=0, has_side_effects=True, vmem_limit_bytes=32 * 2**20
        ),
        cost_estimate=pl.CostEstimate(
            flops=16 * rhs * RANK * points, bytes_accessed=20 * 2**20, transcendentals=0
        ),
        name="tree_solve",
    )(permuted, level_bases, other, capacitance)


def solution(mesh):
    in_specs = (
        P("rep", ("cls", "pts", "sub")),
        P(("cls", "pts", "sub"), None),
        P(None, "rep", ("cls", "pts", "sub")),
        P("cls", None, None),
    )
    out_specs = P("rep", ("cls", "pts", "sub"))
    return jax.shard_map(shards, mesh=mesh, in_specs=in_specs, out_specs=out_specs, check_vma=False)
```

time: 118 us -> 44 us (0.37)
  local copies, waits for them, and re-layouts: 48.8 us -> 7.25 us
  Pallas kernels: 0 us -> 36 us
  matrix products: 29.6 us -> 0 us
  waiting for transfers between devices: 15.5 us -> 0.01 us
  between operations: 13.4 us -> 0.03 us
  starting transfers between devices: 9.18 us -> 0.45 us
  other arithmetic: 1.2 us -> 0 us
    pallas_call x0 -> x2, Pallas kernels: none -> 36 us  [the longest x1 24.3 us: shards(): pl.pallas_call(functools.partial(solve_kernel, levels), out_shape=jax.Sha...]
    gather x2 -> x0, local copies, waits for them, and re-layouts: 31.1 us -> none  [shards(): jnp.take(right_sides, curve_order[0], axis=0 + 1).astype(jnp.float32)]
    dot_general x12 -> x0, matrix products: 29.6 us -> none  [the longest x4 12.8 us: shards(): jnp.einsum('mrk,kmw->rmw', coefficients, level_basis, preferred_element_t...]
    ppermute x6 -> x1, waiting for transfers between devices: 13.6 us -> 0.01 us  [shards(): other = lax.ppermute(level_bases, 'rep', [(0, 1), (1, 0)])]
    ppermute x6 -> x1, starting transfers between devices: 9.06 us -> 0.45 us  [shards(): other = lax.ppermute(level_bases, 'rep', [(0, 1), (1, 0)])]
    unnamed x12 -> x9, local copies, waits for them, and re-layouts: 1.69 us -> 7.25 us
    slice x1 -> x0, local copies, waits for them, and re-layouts: 4.27 us -> none  [shards(): level_bases[tree_level - 1]]
    reshape x2 -> x0, local copies, waits for them, and re-layouts: 4.26 us -> none  [shards(): current = current - update.reshape(rhs_rows, point_count)]
  transfers between devices with their start and end apart: 10 -> 1, of which waited for: 5 -> 0; matrix products, arithmetic and copies ran while one was open for 56% -> 0% of each run, Pallas kernels for 0% -> 27%
where the time goes in v1:
time: 44 us; the launch traced here: 43.7 us
  Pallas kernels  36 us (82%)
  local copies, waits for them, and re-layouts  7.25 us (16%)
  starting transfers between devices  0.45 us (1%)
    pallas_call x1, Pallas kernels, shards(): pl.pallas_call(functools.partial(solve_kernel, levels), out_shape=jax.Sha...  24.3 us
    pallas_call x1, Pallas kernels, gather(): pl.pallas_call(gather_kernel, out_shape=jax.ShapeDtypeStruct((rhs, points...  11.7 us
    unnamed x9, local copies, waits for them, and re-layouts  7.25 us
  transfers between devices with their start and end apart: 1, of which 0 were waited for; matrix products, arithmetic and copies ran while one was open for 0% of the time, Pallas kernels for 27%

profile of v1, /device:TPU:0, one launch (start us, length us, event | category | flops | bytes accessed | tf_op | source)
XLA Modules:
  0.0 43.7 jit_solution(15992084187957063032)
XLA Ops:
  0.0 0.5 %collective-permute-start = (bf16[4,64,8192]{2,1,0:T(8,128)(2,1)}, bf16[4,64,8192]{2,1,0:T(8,128)(2,1)S(1)}, u32[]{:S(2)}, u32[]{:S(2)}) collective-permute-start(bf16[4,64,8192]{2,1,0:T(8,128)(2,1)} %own.1), channel_id=1, source_target_pairs={{0,1},{1,0},{2,3},{3,2},{4,5},{5,4},{6,7},{7,6},{8,9},{9,8},{10,11... | collective-permute-start | bytes 12582920 | tf_op jit(solution)/shard_map/ppermute | solution.py:265
  0.5 0.0 copy-start.2
  0.5 1.2 %copy-done.2 = bf16[64,8192]{1,0:T(8,128)(2,1)S(1)} copy-done((bf16[64,8192]{1,0:T(8,128)(2,1)S(1)}, bf16[64,8192]{1,0:T(8,128)(2,1)}, u32[]{:S(2)}) %copy-start.2) | copy-done | bytes 1048600
  1.7 0.0 copy-start.3
  1.7 0.8 %copy-done.3 = s32[1,8192]{1,0:T(1,128)S(1)} copy-done((s32[1,8192]{1,0:T(1,128)S(1)}, s32[1,8192]{1,0:T(1,128)}, u32[]{:S(2)}) %copy-start.3) | copy-done | bytes 32792
  2.4 11.7 %curve_gather.1.x = bf16[64,8192]{1,0:T(8,128)(2,1)S(1)} custom-call(s32[1,8192]{1,0:T(1,128)S(1)} %copy-done.3, bf16[64,8192]{1,0:T(8,128)(2,1)S(1)} %copy-done.2), custom_call_target="tpu_custom_call" | custom-call | flops 67108864 | bytes 8388608 | tf_op jit(solution)/shard_map/curve_gather/pallas_call | solution.py:58
  14.1 0.0 collective-permute-done.other
  14.1 0.0 copy-start
  14.1 2.2 %copy-done = bf16[4,64,8192]{2,1,0:T(8,128)(2,1)S(1)} copy-done((bf16[4,64,8192]{2,1,0:T(8,128)(2,1)S(1)}, bf16[4,64,8192]{2,1,0:T(8,128)(2,1)}, u32[]{:S(2)}) %copy-start) | copy-done | bytes 4194328
  16.3 0.0 copy-start.1
  16.3 2.1 %copy-done.1 = f32[15,256,256]{2,1,0:T(8,128)S(1)} copy-done((f32[15,256,256]{2,1,0:T(8,128)S(1)}, f32[15,256,256]{2,1,0:T(8,128)}, u32[]{:S(2)}) %copy-start.1) | copy-done | bytes 3932184
  18.4 24.3 %tree_solve.1 = bf16[64,8192]{1,0:T(8,128)(2,1)S(1)} custom-call(bf16[64,8192]{1,0:T(8,128)(2,1)S(1)} %curve_gather.1.x, bf16[4,64,8192]{2,1,0:T(8,128)(2,1)S(1)} %copy-done, bf16[4,64,8192]{2,1,0:T(8,128)(2,1)S(1)} %collective-permute-done.other, f32[15,256,256]{2,1,0:T(8,128)S(1)} %copy-done.1), custom_call_target="tpu_custom_call" | custom-call | flops 1073741824 | bytes 20971520 | tf_op jit(solution)/shard_map/tree_solve/pallas_call | solution.py:269
  42.8 1.0 %copy.6 = bf16[64,8192]{1,0:T(8,128)(2,1)} copy(bf16[64,8192]{1,0:T(8,128)(2,1)S(1)} %tree_solve.1) | data formatting | bytes 2097152
Async XLA Ops:
  0.0 14.1 %collective-permute-start = (bf16[4,64,8192]{2,1,0:T(8,128)(2,1)}, bf16[4,64,8192]{2,1,0:T(8,128)(2,1)S(1)}, u32[]{:S(2)}, u32[]{:S(2)}) collective-permute-start(bf16[4,64,8192]{2,1,0:T(8,128)(2,1)} %own.1), channel_id=1, source_target_pairs={{0,1},{1,0},{2,3},{3,2},{4,5},{5,4},{6,7},{7,6},{8,9},{9,8},{10,11... | collective-permute-start | bytes 12582920 | tf_op jit(solution)/shard_map/ppermute | solution.py:265
  0.5 1.2 %copy-start.2 = (bf16[64,8192]{1,0:T(8,128)(2,1)S(1)}, bf16[64,8192]{1,0:T(8,128)(2,1)}, u32[]{:S(2)}) copy-start(bf16[64,8192]{1,0:T(8,128)(2,1)} %x.1) | copy-start | bytes 3145732
  1.7 0.8 %copy-start.3 = (s32[1,8192]{1,0:T(1,128)S(1)}, s32[1,8192]{1,0:T(1,128)}, u32[]{:S(2)}) copy-start(s32[1,8192]{1,0:T(1,128)} %order.1) | copy-start | bytes 98308
  14.1 2.2 %copy-start = (bf16[4,64,8192]{2,1,0:T(8,128)(2,1)S(1)}, bf16[4,64,8192]{2,1,0:T(8,128)(2,1)}, u32[]{:S(2)}) copy-start(bf16[4,64,8192]{2,1,0:T(8,128)(2,1)} %own.1) | copy-start | bytes 12582916
  16.3 2.1 %copy-start.1 = (f32[15,256,256]{2,1,0:T(8,128)S(1)}, f32[15,256,256]{2,1,0:T(8,128)}, u32[]{:S(2)}) copy-start(f32[15,256,256]{2,1,0:T(8,128)} %cap.1) | copy-start | bytes 11796484

commit v2 on v1

--- a/solution.py
+++ b/solution.py
@@ -11,7 +11,8 @@
 RANK = 128
 LEVELS = 4
 LANES = 128
-CHUNK = 2048
+CHUNK = 1024
+PIECES = 4
 STAGE_BITS = 2
 MESH = pl.DeviceIdType.MESH
 F32 = jnp.float32
@@ -20,60 +21,6 @@
 
 def dot_nt(a, b):
     return lax.dot_general(a, b, (((1,), (1,)), ((), ())), preferred_element_type=F32)
-
-
-def gather_kernel(order, x, out, table, rows_a, rows_b):
-    rhs, points = x.shape
-    blocks = points // LANES
-
-    @pl.loop(0, blocks, unroll=4)
-    def _(b):
-        cols = pl.ds(pl.multiple_of(b * LANES, LANES), LANES)
-        table[cols, 0:rhs] = x[:, cols].astype(F32).T
-
-    def pick(b, rows):
-        for j in range(LANES):
-            rows[pl.ds(j, 1), :] = table[pl.ds(order[0, b * LANES + j], 1), :]
-
-    def put(b, rows):
-        cols = pl.ds(pl.multiple_of(b * LANES, LANES), LANES)
-        out[:, cols] = rows[...].T[0:rhs].astype(BF16)
-
-    pick(0, rows_a)
-
-    @pl.loop(0, blocks // 2 - 1)
-    def _(i):
-        pick(2 * i + 1, rows_b)
-        put(2 * i, rows_a)
-        pick(2 * i + 2, rows_a)
-        put(2 * i + 1, rows_b)
-
-    pick(blocks - 1, rows_b)
-    put(blocks - 2, rows_a)
-    put(blocks - 1, rows_b)
-
-
-def gather(order, x):
-    rhs, points = x.shape
-    return pl.pallas_call(
-        gather_kernel,
-        out_shape=jax.ShapeDtypeStruct((rhs, points), BF16),
-        in_specs=[
-            pl.BlockSpec(memory_space=pltpu.SMEM),
-            pl.BlockSpec(memory_space=pltpu.VMEM),
-        ],
-        out_specs=pl.BlockSpec(memory_space=pltpu.VMEM),
-        scratch_shapes=[
-            pltpu.VMEM((points, LANES), F32),
-            pltpu.VMEM((LANES, LANES), F32),
-            pltpu.VMEM((LANES, LANES), F32),
-        ],
-        compiler_params=pltpu.CompilerParams(vmem_limit_bytes=24 * 2**20),
-        cost_estimate=pl.CostEstimate(
-            flops=points * LANES * 64, bytes_accessed=16 * rhs * points, transcendentals=0
-        ),
-        name="curve_gather",
-    )(order, x)
 
 
 def plan(points, total):
@@ -103,11 +50,38 @@
     return high, (value - high.astype(F32)).astype(BF16)
 
 
+def gather(order, x, out, table, rows_a, rows_b):
+    rhs, points = x.shape
+    blocks = points // LANES
+
+    def pick(b, rows):
+        for j in range(LANES):
+            rows[pl.ds(j, 1), :] = table[pl.ds(order[0, b * LANES + j], 1), :]
+
+    def put(b, rows):
+        cols = pl.ds(pl.multiple_of(b * LANES, LANES), LANES)
+        out[:, cols] = rows[...].T[0:rhs].astype(BF16)
+
+    pick(0, rows_a)
+
+    @pl.loop(0, blocks // 2 - 1)
+    def _(i):
+        pick(2 * i + 1, rows_b)
+        put(2 * i, rows_a)
+        pick(2 * i + 2, rows_a)
+        put(2 * i + 1, rows_b)
+
+    pick(blocks - 1, rows_b)
+    put(blocks - 2, rows_a)
+    put(blocks - 1, rows_b)
+
+
 def solve_kernel(
-    levels, x, own, other, cap, out, current, basis, caps, send, recv,
-    basis_sems, cap_sems, send_sems, recv_sems,
+    levels, sides, order_in, own, cap, out,
+    raw, order, x, table, rows_a, rows_b, current, basis, caps, result, send, recv,
+    in_sems, basis_sems, far_send_sems, far_recv_sems, cap_sems, out_sems, send_sems, recv_sems,
 ):
-    rhs, points = x.shape
+    rhs, points = raw.shape
     half = own.shape[1]
     sub_size = lax.axis_size("sub")
     sub_bits = sub_size.bit_length() - 1
@@ -126,25 +100,37 @@
 
     masks = sorted({m for _, _, _, stages, _ in levels for stage in stages for m, _, _ in stage})
     barrier = pltpu.get_barrier_semaphore()
+    pl.semaphore_signal(barrier, inc=1, device_id={"rep": 1 - rep}, device_id_type=MESH)
     for mask in masks:
         pl.semaphore_signal(barrier, inc=1, device_id=partner(mask), device_id_type=MESH)
+
+    piece_width = points // PIECES
+    side_copies = []
+    for piece in range(PIECES):
+        cols = pl.ds(piece * piece_width, piece_width)
+        side_copies.append(
+            pltpu.make_async_copy(sides.at[:, cols], raw.at[:, cols], in_sems.at[piece])
+        )
+        side_copies[-1].start()
+    order_copy = pltpu.make_async_copy(order_in, order, in_sems.at[PIECES])
+    order_copy.start()
 
     basis_copies, cap_copies = [], []
     for n, (level, span, local, _, _) in enumerate(levels):
         first = block // span * local
         parent = 2 ** (level - 1) - 1 + first // 2
         odd = first % 2
-        copies = []
-        for piece, source in enumerate((own, other)):
-            row = rep * half if piece == 0 else (1 - rep) * half
-            copies.append(
-                pltpu.make_async_copy(
-                    source.at[level - 1],
-                    basis.at[n, pl.ds(pl.multiple_of(row, half), half), :],
-                    basis_sems.at[n, piece],
-                )
-            )
-        basis_copies.append(copies)
+        mine_at = basis.at[n, pl.ds(pl.multiple_of(rep * half, half), half), :]
+        here = pltpu.make_async_copy(own.at[level - 1], mine_at, basis_sems.at[n])
+        far = pltpu.make_async_remote_copy(
+            src_ref=own.at[level - 1],
+            dst_ref=mine_at,
+            send_sem=far_send_sems.at[n],
+            recv_sem=far_recv_sems.at[n],
+            device_id={"rep": 1 - rep},
+            device_id_type=MESH,
+        )
+        basis_copies.append((here, far))
         if local == 1:
             mine = pl.ds(pl.multiple_of(odd * RANK, RANK), RANK)
             theirs = pl.ds(pl.multiple_of((1 - odd) * RANK, RANK), RANK)
@@ -160,8 +146,22 @@
             )
         else:
             cap_copies.append([pltpu.make_async_copy(cap.at[parent], caps.at[n], cap_sems.at[n, 0])])
-        for copy in copies + cap_copies[-1]:
+        for copy in [here] + cap_copies[-1]:
             copy.start()
+
+    for piece in range(PIECES):
+        side_copies[piece].wait()
+
+        @pl.loop(piece * piece_width // LANES, (piece + 1) * piece_width // LANES, unroll=4)
+        def _(b):
+            cols = pl.ds(pl.multiple_of(b * LANES, LANES), LANES)
+            table[cols, 0:rhs] = raw[:, cols].astype(F32).T
+
+    pl.semaphore_wait(barrier, len(masks) + 1)
+    for _, far in basis_copies:
+        far.start()
+    order_copy.wait()
+    gather(order, raw, x, table, rows_a, rows_b)
 
     def chunk(i):
         return pl.ds(pl.multiple_of(i * CHUNK, CHUNK), CHUNK)
@@ -186,7 +186,6 @@
             )
         )
 
-    barrier_waited = False
     for n, (level, span, local, stages, factor) in enumerate(levels):
         for copy in cap_copies[n]:
             copy.wait()
@@ -198,9 +197,6 @@
             sibling = None
             c = caps[n, 0:RANK, :]
             for stage in stages:
-                if not barrier_waited:
-                    pl.semaphore_wait(barrier, len(masks))
-                    barrier_waited = True
                 slot0 = stage[0][2]
                 send[slot0] = total.astype(BF16)
                 copies = []
@@ -244,52 +240,72 @@
                 update = jnp.dot(mine, basis[n, :, here], preferred_element_type=F32)
                 value = before[:, here].astype(F32) - update
                 if last:
-                    out[:, here] = value.astype(BF16)
+                    result[:, here] = value.astype(BF16)
                     return total
                 current[:, here] = value
                 return total + dot_nt(value.astype(BF16), basis[n + 1, :, here])
 
+            if last:
+                out_copies = []
+                for part in range(PIECES):
+                    for i in range(part * steps // PIECES, (part + 1) * steps // PIECES):
+                        step(i, None)
+                    cols = pl.ds(part * piece_width, piece_width)
+                    out_copies.append(
+                        pltpu.make_async_copy(result.at[:, cols], out.at[:, cols], out_sems.at[part])
+                    )
+                    out_copies[-1].start()
+                for copy in out_copies:
+                    copy.wait()
+                return
             total = lax.fori_loop(
                 piece * width, (piece + 1) * width, step, jnp.zeros((rhs, RANK), F32)
             )
             sums.append(total)
-        if not last:
-            group = pieces // next_local
-            sums = [sum(sums[i * group + 1 : (i + 1) * group], sums[i * group]) for i in range(next_local)]
+        group = pieces // next_local
+        sums = [sum(sums[i * group + 1 : (i + 1) * group], sums[i * group]) for i in range(next_local)]
 
 
 def shards(right_sides, curve_order, level_bases, capacitance):
     rhs, points = right_sides.shape
     total = points * lax.axis_size(("pts", "sub"))
     levels, slots = plan(points, total)
-    other = lax.ppermute(level_bases, "rep", [(0, 1), (1, 0)])
-    permuted = gather(curve_order, right_sides)
-    hbm = pl.BlockSpec(memory_space=pl.ANY)
-    vmem = pl.BlockSpec(memory_space=pltpu.VMEM)
+    hbm = pl.BlockSpec(memory_space=pltpu.MemorySpace.HBM)
     return pl.pallas_call(
         functools.partial(solve_kernel, levels),
         out_shape=jax.ShapeDtypeStruct((rhs, points), BF16),
-        in_specs=[vmem, hbm, hbm, hbm],
-        out_specs=vmem,
+        in_specs=[hbm, hbm, hbm, hbm],
+        out_specs=hbm,
         scratch_shapes=[
+            pltpu.VMEM((rhs, points), BF16),
+            pltpu.SMEM((1, points), jnp.int32),
+            pltpu.VMEM((rhs, points), BF16),
+            pltpu.VMEM((points, LANES), F32),
+            pltpu.VMEM((LANES, LANES), F32),
+            pltpu.VMEM((LANES, LANES), F32),
             pltpu.VMEM((rhs, points), F32),
             pltpu.VMEM((LEVELS, RANK, points), BF16),
             pltpu.VMEM((LEVELS, 2 * RANK, 2 * RANK), F32),
+            pltpu.VMEM((rhs, points), BF16),
             pltpu.VMEM((slots, rhs, RANK), BF16),
             pltpu.VMEM((slots, rhs, RANK), BF16),
+            pltpu.SemaphoreType.DMA((PIECES + 1,)),
+            pltpu.SemaphoreType.DMA((LEVELS,)),
+            pltpu.SemaphoreType.DMA((LEVELS,)),
+            pltpu.SemaphoreType.DMA((LEVELS,)),
             pltpu.SemaphoreType.DMA((LEVELS, 2)),
-            pltpu.SemaphoreType.DMA((LEVELS, 2)),
+            pltpu.SemaphoreType.DMA((PIECES,)),
             pltpu.SemaphoreType.DMA((slots,)),
             pltpu.SemaphoreType.DMA((slots,)),
         ],
         compiler_params=pltpu.CompilerParams(
-            collective_id=0, has_side_effects=True, vmem_limit_bytes=32 * 2**20
+            collective_id=0, has_side_effects=True, vmem_limit_bytes=48 * 2**20
         ),
         cost_estimate=pl.CostEstimate(
             flops=16 * rhs * RANK * points, bytes_accessed=20 * 2**20, transcendentals=0
         ),
         name="tree_solve",
-    )(permuted, level_bases, other, capacitance)
+    )(right_sides, curve_order, level_bases, capacitance)
 
 
 def solution(mesh):

time: 44 us -> 43.7 us (level)
  Pallas kernels: 36 us -> 38.4 us
  local copies, waits for them, and re-layouts: 7.25 us -> 5.07 us
  starting transfers between devices: 0.45 us -> 0 us
    pallas_call x1, Pallas kernels: 24.3 us -> 38.4 us  [shards(): pl.pallas_call(functools.partial(solve_kernel, levels), out_shape=jax.Sha...]
    pallas_call x1 -> x0, Pallas kernels: 11.7 us -> none  [gather(): pl.pallas_call(gather_kernel, out_shape=jax.ShapeDtypeStruct((rhs, points...]
    unnamed x9 -> x7, local copies, waits for them, and re-layouts: 7.25 us -> 5.07 us
    ppermute x1 -> x0, starting transfers between devices: 0.45 us -> none  [shards(): other = lax.ppermute(level_bases, 'rep', [(0, 1), (1, 0)])]
  transfers between devices with their start and end apart: 1 -> 0, of which waited for: 0 -> 0; matrix products, arithmetic and copies ran while one was open for 0% -> 0% of each run, Pallas kernels for 27% -> 0%
where the time goes in v2:
time: 43.7 us; the launch traced here: 43.4 us
  Pallas kernels  38.4 us (88%)
  local copies, waits for them, and re-layouts  5.07 us (12%)
    pallas_call x1, Pallas kernels, shards(): pl.pallas_call(functools.partial(solve_kernel, levels), out_shape=jax.Sha...  38.4 us
    unnamed x7, local copies, waits for them, and re-layouts  5.07 us

profile of v2, /device:TPU:0, one launch (start us, length us, event | category | flops | bytes accessed | tf_op | source)
XLA Modules:
  0.0 43.4 jit_solution(8796421415378125042)
XLA Ops:
  0.0 0.0 copy-start
  0.0 2.1 %copy-done = f32[15,256,256]{2,1,0:T(8,128)S(1)} copy-done((f32[15,256,256]{2,1,0:T(8,128)S(1)}, f32[15,256,256]{2,1,0:T(8,128)}, u32[]{:S(2)}) %copy-start) | copy-done | bytes 3932184
  2.1 0.0 copy-start.1
  2.1 1.2 %copy-done.1 = bf16[64,8192]{1,0:T(8,128)(2,1)S(1)} copy-done((bf16[64,8192]{1,0:T(8,128)(2,1)S(1)}, bf16[64,8192]{1,0:T(8,128)(2,1)}, u32[]{:S(2)}) %copy-start.1) | copy-done | bytes 1048600
  3.3 0.0 copy-start.2
  3.3 0.8 %copy-done.2 = s32[1,8192]{1,0:T(1,128)S(1)} copy-done((s32[1,8192]{1,0:T(1,128)S(1)}, s32[1,8192]{1,0:T(1,128)}, u32[]{:S(2)}) %copy-start.2) | copy-done | bytes 32792
  4.1 38.4 %tree_solve.1 = bf16[64,8192]{1,0:T(8,128)(2,1)S(1)} custom-call(bf16[64,8192]{1,0:T(8,128)(2,1)S(1)} %copy-done.1, s32[1,8192]{1,0:T(1,128)S(1)} %copy-done.2, bf16[4,64,8192]{2,1,0:T(8,128)(2,1)} %own.1, f32[15,256,256]{2,1,0:T(8,128)S(1)} %copy-done), custom_call_target="tpu_custom_call" | custom-call | flops 1073741824 | bytes 20971520 | tf_op jit(solution)/shard_map/tree_solve/pallas_call | solution.py:274
  42.5 1.0 %copy.6 = bf16[64,8192]{1,0:T(8,128)(2,1)} copy(bf16[64,8192]{1,0:T(8,128)(2,1)S(1)} %tree_solve.1) | data formatting | bytes 2097152
Async XLA Ops:
  0.0 2.1 %copy-start = (f32[15,256,256]{2,1,0:T(8,128)S(1)}, f32[15,256,256]{2,1,0:T(8,128)}, u32[]{:S(2)}) copy-start(f32[15,256,256]{2,1,0:T(8,128)} %cap.1) | copy-start | bytes 11796484
  2.1 1.2 %copy-start.1 = (bf16[64,8192]{1,0:T(8,128)(2,1)S(1)}, bf16[64,8192]{1,0:T(8,128)(2,1)}, u32[]{:S(2)}) copy-start(bf16[64,8192]{1,0:T(8,128)(2,1)} %sides.1) | copy-start | bytes 3145732
  3.3 0.8 %copy-start.2 = (s32[1,8192]{1,0:T(1,128)S(1)}, s32[1,8192]{1,0:T(1,128)}, u32[]{:S(2)}) copy-start(s32[1,8192]{1,0:T(1,128)} %order_in.1) | copy-start | bytes 98308

commit v3 on v2

--- a/solution.py
+++ b/solution.py
@@ -50,9 +50,8 @@
     return high, (value - high.astype(F32)).astype(BF16)
 
 
-def gather(order, x, out, table, rows_a, rows_b):
-    rhs, points = x.shape
-    blocks = points // LANES
+def gather(order, x, out, table, rows_a, rows_b, first, stop):
+    rhs = x.shape[0]
 
     def pick(b, rows):
         for j in range(LANES):
@@ -62,18 +61,18 @@
         cols = pl.ds(pl.multiple_of(b * LANES, LANES), LANES)
         out[:, cols] = rows[...].T[0:rhs].astype(BF16)
 
-    pick(0, rows_a)
-
-    @pl.loop(0, blocks // 2 - 1)
+    pick(first, rows_a)
+
+    @pl.loop(first // 2, stop // 2 - 1)
     def _(i):
         pick(2 * i + 1, rows_b)
         put(2 * i, rows_a)
         pick(2 * i + 2, rows_a)
         put(2 * i + 1, rows_b)
 
-    pick(blocks - 1, rows_b)
-    put(blocks - 2, rows_a)
-    put(blocks - 1, rows_b)
+    pick(stop - 1, rows_b)
+    put(stop - 2, rows_a)
+    put(stop - 1, rows_b)
 
 
 def solve_kernel(
@@ -149,6 +148,15 @@
         for copy in [here] + cap_copies[-1]:
             copy.start()
 
+    def share_basis():
+        pl.semaphore_wait(barrier, len(masks) + 1)
+        for _, far in basis_copies:
+            far.start()
+
+    @pl.when(rep != 0)
+    def _():
+        share_basis()
+
     for piece in range(PIECES):
         side_copies[piece].wait()
 
@@ -157,11 +165,14 @@
             cols = pl.ds(pl.multiple_of(b * LANES, LANES), LANES)
             table[cols, 0:rhs] = raw[:, cols].astype(F32).T
 
-    pl.semaphore_wait(barrier, len(masks) + 1)
-    for _, far in basis_copies:
-        far.start()
     order_copy.wait()
-    gather(order, raw, x, table, rows_a, rows_b)
+    gather(order, raw, x, table, rows_a, rows_b, 0, points // LANES // 2)
+
+    @pl.when(rep == 0)
+    def _():
+        share_basis()
+
+    gather(order, raw, x, table, rows_a, rows_b, points // LANES // 2, points // LANES)
 
     def chunk(i):
         return pl.ds(pl.multiple_of(i * CHUNK, CHUNK), CHUNK)
@@ -299,7 +310,7 @@
             pltpu.SemaphoreType.DMA((slots,)),
         ],
         compiler_params=pltpu.CompilerParams(
-            collective_id=0, has_side_effects=True, vmem_limit_bytes=48 * 2**20
+            collective_id=0, has_side_effects=True, vmem_limit_bytes=62 * 2**20
         ),
         cost_estimate=pl.CostEstimate(
             flops=16 * rhs * RANK * points, bytes_accessed=20 * 2**20, transcendentals=0

time: 43.7 us -> 42 us (0.961)
  local copies, waits for them, and re-layouts: 5.07 us -> 2.26 us
  Pallas kernels: 38.4 us -> 39.6 us
    unnamed x7 -> x1, local copies, waits for them, and re-layouts: 5.07 us -> 2.26 us
    pallas_call x1, Pallas kernels: 38.4 us -> 39.6 us  [shards(): pl.pallas_call(functools.partial(solve_kernel, levels), out_shape=jax.Sha...]
where the time goes in v3:
time: 42 us; the launch traced here: 41.8 us
  Pallas kernels  39.6 us (94%)
  local copies, waits for them, and re-layouts  2.26 us (5%)
    pallas_call x1, Pallas kernels, shards(): pl.pallas_call(functools.partial(solve_kernel, levels), out_shape=jax.Sha...  39.6 us
    unnamed x1, local copies, waits for them, and re-layouts  2.26 us

profile of v3, /device:TPU:0, one launch (start us, length us, event | category | flops | bytes accessed | tf_op | source)
XLA Modules:
  0.0 41.8 jit_solution(15032481129080965160)
XLA Ops:
  0.0 39.6 %tree_solve.1 = bf16[64,8192]{1,0:T(8,128)(2,1)} custom-call(bf16[64,8192]{1,0:T(8,128)(2,1)} %sides.1, s32[1,8192]{1,0:T(1,128)} %order_in.1, bf16[4,64,8192]{2,1,0:T(8,128)(2,1)} %own.1, f32[15,256,256]{2,1,0:T(8,128)} %cap.1), custom_call_target="tpu_custom_call" | custom-call | flops 1073741824 | bytes 20971520 | tf_op jit(solution)/shard_map/tree_solve/pallas_call | solution.py:285
  39.6 2.3 %copy.6 = bf16[64,8192]{1,0:T(8,128)(2,1)} copy(bf16[64,8192]{1,0:T(8,128)(2,1)} %tree_solve.1) | data formatting | bytes 2097152

commit v4 on v3

--- a/solution.py
+++ b/solution.py
@@ -59,7 +59,7 @@
 
     def put(b, rows):
         cols = pl.ds(pl.multiple_of(b * LANES, LANES), LANES)
-        out[:, cols] = rows[...].T[0:rhs].astype(BF16)
+        out[:, cols] = rows[...].astype(BF16).T[0:rhs]
 
     pick(first, rows_a)
 
@@ -77,8 +77,8 @@
 
 def solve_kernel(
     levels, sides, order_in, own, cap, out,
-    raw, order, x, table, rows_a, rows_b, current, basis, caps, result, send, recv,
-    in_sems, basis_sems, far_send_sems, far_recv_sems, cap_sems, out_sems, send_sems, recv_sems,
+    raw, order, x, table, rows_a, rows_b, current, basis, caps, send, recv,
+    in_sems, basis_sems, far_send_sems, far_recv_sems, cap_sems, send_sems, recv_sems,
 ):
     rhs, points = raw.shape
     half = own.shape[1]
@@ -163,7 +163,7 @@
         @pl.loop(piece * piece_width // LANES, (piece + 1) * piece_width // LANES, unroll=4)
         def _(b):
             cols = pl.ds(pl.multiple_of(b * LANES, LANES), LANES)
-            table[cols, 0:rhs] = raw[:, cols].astype(F32).T
+            table[cols, 0:rhs] = raw[:, cols].T.astype(F32)
 
     order_copy.wait()
     gather(order, raw, x, table, rows_a, rows_b, 0, points // LANES // 2)
@@ -197,7 +197,29 @@
             )
         )
 
+    def sweep(n, source, pending):
+        ahead = n + 1 < LEVELS
+        if ahead:
+            wait_basis(n + 1)
+
+        def step(i, total):
+            here = chunk(i)
+            value = source[:, here]
+            if pending is not None:
+                value = value - jnp.dot(
+                    pending, basis[n - 1, :, here], preferred_element_type=F32
+                )
+                current[:, here] = value
+            if not ahead:
+                return total
+            left = jnp.concatenate([value.astype(BF16), basis[n, :, here]], axis=0)
+            return total + dot_nt(left, basis[n + 1, :, here])
+
+        return lax.fori_loop(0, steps, step, jnp.zeros((rhs + RANK, RANK), F32))
+
+    source, pending = x, None
     for n, (level, span, local, stages, factor) in enumerate(levels):
+        last = n == LEVELS - 1
         for copy in cap_copies[n]:
             copy.wait()
         if local > 1:
@@ -207,7 +229,7 @@
             total = sums[0]
             sibling = None
             c = caps[n, 0:RANK, :]
-            for stage in stages:
+            for at, stage in enumerate(stages):
                 slot0 = stage[0][2]
                 send[slot0] = total.astype(BF16)
                 copies = []
@@ -222,6 +244,10 @@
                     )
                     copy.start()
                     copies.append(copy)
+                if at == 0:
+                    products = sweep(n, source, pending)
+                    if pending is not None:
+                        source = current
                 for copy, (mask, crosses, slot) in zip(copies, stage):
                     copy.wait()
                     value = recv[slot].astype(F32)
@@ -234,46 +260,38 @@
         s_high, s_low = split(s)
         coefficients = dot_nt(s_high, c_high) + dot_nt(s_low, c_high) + dot_nt(s_high, c_low)
         coefficients = (coefficients * factor).astype(BF16)
-        before = x if n == 0 else current
-        last = n == LEVELS - 1
-        if not last:
-            wait_basis(n + 1)
-            next_local = levels[n + 1][2]
-        pieces = max(local, 1 if last else next_local)
-        width = steps // pieces
+        if local == 1 and not last:
+            g_high, g_low = split(products[rhs:])
+            change = jnp.dot(coefficients, g_high, preferred_element_type=F32)
+            change = change + jnp.dot(coefficients, g_low, preferred_element_type=F32)
+            sums = [products[0:rhs] - change]
+            pending = coefficients
+            continue
+        if local == 1:
+            for i in range(steps):
+                here = chunk(i)
+                update = jnp.dot(coefficients, basis[n, :, here], preferred_element_type=F32)
+                out[:, here] = (source[:, here].astype(F32) - update).astype(BF16)
+            return
+        wait_basis(n + 1)
+        next_local = levels[n + 1][2]
+        width = steps // local
         sums = []
-        for piece in range(pieces):
-            node = piece * local // pieces
+        for node in range(local):
             mine = coefficients[:, node * RANK : (node + 1) * RANK]
 
             def step(i, total):
                 here = chunk(i)
                 update = jnp.dot(mine, basis[n, :, here], preferred_element_type=F32)
-                value = before[:, here].astype(F32) - update
-                if last:
-                    result[:, here] = value.astype(BF16)
-                    return total
+                value = source[:, here].astype(F32) - update
                 current[:, here] = value
                 return total + dot_nt(value.astype(BF16), basis[n + 1, :, here])
 
-            if last:
-                out_copies = []
-                for part in range(PIECES):
-                    for i in range(part * steps // PIECES, (part + 1) * steps // PIECES):
-                        step(i, None)
-                    cols = pl.ds(part * piece_width, piece_width)
-                    out_copies.append(
-                        pltpu.make_async_copy(result.at[:, cols], out.at[:, cols], out_sems.at[part])
-                    )
-                    out_copies[-1].start()
-                for copy in out_copies:
-                    copy.wait()
-                return
-            total = lax.fori_loop(
-                piece * width, (piece + 1) * width, step, jnp.zeros((rhs, RANK), F32)
+            sums.append(
+                lax.fori_loop(node * width, (node + 1) * width, step, jnp.zeros((rhs, RANK), F32))
             )
-            sums.append(total)
-        group = pieces // next_local
+        source = current
+        group = local // next_local
         sums = [sum(sums[i * group + 1 : (i + 1) * group], sums[i * group]) for i in range(next_local)]
 
 
@@ -286,7 +304,7 @@
         functools.partial(solve_kernel, levels),
         out_shape=jax.ShapeDtypeStruct((rhs, points), BF16),
         in_specs=[hbm, hbm, hbm, hbm],
-        out_specs=hbm,
+        out_specs=pl.BlockSpec(memory_space=pltpu.VMEM),
         scratch_shapes=[
             pltpu.VMEM((rhs, points), BF16),
             pltpu.SMEM((1, points), jnp.int32),
@@ -297,7 +315,6 @@
             pltpu.VMEM((rhs, points), F32),
             pltpu.VMEM((LEVELS, RANK, points), BF16),
             pltpu.VMEM((LEVELS, 2 * RANK, 2 * RANK), F32),
-            pltpu.VMEM((rhs, points), BF16),
             pltpu.VMEM((slots, rhs, RANK), BF16),
             pltpu.VMEM((slots, rhs, RANK), BF16),
             pltpu.SemaphoreType.DMA((PIECES + 1,)),
@@ -305,12 +322,11 @@
             pltpu.SemaphoreType.DMA((LEVELS,)),
             pltpu.SemaphoreType.DMA((LEVELS,)),
             pltpu.SemaphoreType.DMA((LEVELS, 2)),
-            pltpu.SemaphoreType.DMA((PIECES,)),
             pltpu.SemaphoreType.DMA((slots,)),
             pltpu.SemaphoreType.DMA((slots,)),
         ],
         compiler_params=pltpu.CompilerParams(
-            collective_id=0, has_side_effects=True, vmem_limit_bytes=62 * 2**20
+            collective_id=0, has_side_effects=True, vmem_limit_bytes=61 * 2**20
         ),
         cost_estimate=pl.CostEstimate(
             flops=16 * rhs * RANK * points, bytes_accessed=20 * 2**20, transcendentals=0

time: 42 us -> 36.8 us (0.88)
  Pallas kernels: 39.6 us -> 34.4 us
    pallas_call x1, Pallas kernels: 39.6 us -> 34.4 us  [shards(): pl.pallas_call(functools.partial(solve_kernel, levels), out_shape=jax.Sha...]
where the time goes in v4:
time: 36.8 us; the launch traced here: 36.7 us
  Pallas kernels  34.4 us (93%)
  local copies, waits for them, and re-layouts  2.26 us (6%)
    pallas_call x1, Pallas kernels, shards(): pl.pallas_call(functools.partial(solve_kernel, levels), out_shape=jax.Sha...  34.4 us
    unnamed x1, local copies, waits for them, and re-layouts  2.26 us

profile of v4, /device:TPU:0, one launch (start us, length us, event | category | flops | bytes accessed | tf_op | source)
XLA Modules:
  0.0 36.7 jit_solution(1635443672621167490)
XLA Ops:
  0.0 34.4 %tree_solve.1 = bf16[64,8192]{1,0:T(8,128)(2,1)} custom-call(bf16[64,8192]{1,0:T(8,128)(2,1)} %sides.1, s32[1,8192]{1,0:T(1,128)} %order_in.1, bf16[4,64,8192]{2,1,0:T(8,128)(2,1)} %own.1, f32[15,256,256]{2,1,0:T(8,128)} %cap.1), custom_call_target="tpu_custom_call" | custom-call | flops 1073741824 | bytes 20971520 | tf_op jit(solution)/shard_map/tree_solve/pallas_call | solution.py:303
  34.4 2.3 %copy.6 = bf16[64,8192]{1,0:T(8,128)(2,1)} copy(bf16[64,8192]{1,0:T(8,128)(2,1)} %tree_solve.1) | data formatting | bytes 2097152

commit v5 on v4

--- a/solution.py
+++ b/solution.py
@@ -53,9 +53,12 @@
 def gather(order, x, out, table, rows_a, rows_b, first, stop):
     rhs = x.shape[0]
 
+    table_rows = table.reshape(table.shape[0], 1, LANES)
+
     def pick(b, rows):
+        picked = rows.reshape(LANES, 1, LANES)
         for j in range(LANES):
-            rows[pl.ds(j, 1), :] = table[pl.ds(order[0, b * LANES + j], 1), :]
+            picked[j] = table_rows[order[0, b * LANES + j]]
 
     def put(b, rows):
         cols = pl.ds(pl.multiple_of(b * LANES, LANES), LANES)
@@ -326,7 +329,7 @@
             pltpu.SemaphoreType.DMA((slots,)),
         ],
         compiler_params=pltpu.CompilerParams(
-            collective_id=0, has_side_effects=True, vmem_limit_bytes=61 * 2**20
+            collective_id=0, has_side_effects=True, vmem_limit_bytes=60 * 2**20
         ),
         cost_estimate=pl.CostEstimate(
             flops=16 * rhs * RANK * points, bytes_accessed=20 * 2**20, transcendentals=0

time: 36.8 us -> 36.8 us (level)
  no operation moved by 1% of the time
where the time goes in v5:
time: 36.8 us; the launch traced here: 36.7 us
  Pallas kernels  34.4 us (93%)
  local copies, waits for them, and re-layouts  2.26 us (6%)
    pallas_call x1, Pallas kernels, shards(): pl.pallas_call(functools.partial(solve_kernel, levels), out_shape=jax.Sha...  34.4 us
    unnamed x1, local copies, waits for them, and re-layouts  2.26 us

profile of v5, /device:TPU:0, one launch (start us, length us, event | category | flops | bytes accessed | tf_op | source)
XLA Modules:
  0.0 36.7 jit_solution(1635443672621167490)
XLA Ops:
  0.0 34.4 %tree_solve.1 = bf16[64,8192]{1,0:T(8,128)(2,1)} custom-call(bf16[64,8192]{1,0:T(8,128)(2,1)} %sides.1, s32[1,8192]{1,0:T(1,128)} %order_in.1, bf16[4,64,8192]{2,1,0:T(8,128)(2,1)} %own.1, f32[15,256,256]{2,1,0:T(8,128)} %cap.1), custom_call_target="tpu_custom_call" | custom-call | flops 1073741824 | bytes 20971520 | tf_op jit(solution)/shard_map/tree_solve/pallas_call | solution.py:306
  34.4 2.3 %copy.6 = bf16[64,8192]{1,0:T(8,128)(2,1)} copy(bf16[64,8192]{1,0:T(8,128)(2,1)} %tree_solve.1) | data formatting | bytes 2097152

commit v6 on v5

--- a/solution.py
+++ b/solution.py
@@ -50,7 +50,7 @@
     return high, (value - high.astype(F32)).astype(BF16)
 
 
-def gather(order, x, out, table, rows_a, rows_b, first, stop):
+def gather(order, x, out, table, rows_a, rows_b, first, stop, beside=None, carry=None):
     rhs = x.shape[0]
 
     table_rows = table.reshape(table.shape[0], 1, LANES)
@@ -66,16 +66,22 @@
 
     pick(first, rows_a)
 
-    @pl.loop(first // 2, stop // 2 - 1)
-    def _(i):
+    def step(i, carry):
         pick(2 * i + 1, rows_b)
         put(2 * i, rows_a)
+        if beside is not None:
+            carry = beside(i - first // 2, carry)
         pick(2 * i + 2, rows_a)
         put(2 * i + 1, rows_b)
-
+        return carry
+
+    carry = lax.fori_loop(first // 2, stop // 2 - 1, step, carry)
     pick(stop - 1, rows_b)
     put(stop - 2, rows_a)
+    if beside is not None:
+        carry = beside((stop - first) // 2 - 1, carry)
     put(stop - 1, rows_b)
+    return carry
 
 
 def solve_kernel(
@@ -169,36 +175,47 @@
             table[cols, 0:rhs] = raw[:, cols].T.astype(F32)
 
     order_copy.wait()
-    gather(order, raw, x, table, rows_a, rows_b, 0, points // LANES // 2)
+    def chunk(i):
+        return pl.ds(pl.multiple_of(i * CHUNK, CHUNK), CHUNK)
+
+    steps = points // CHUNK
+
+    def wait_basis(n):
+        for copy in basis_copies[n]:
+            copy.wait()
+
+    blocks = points // LANES
+    local = levels[0][2]
+    gather(order, raw, x, table, rows_a, rows_b, 0, blocks // 4)
 
     @pl.when(rep == 0)
     def _():
         share_basis()
 
-    gather(order, raw, x, table, rows_a, rows_b, points // LANES // 2, points // LANES)
-
-    def chunk(i):
-        return pl.ds(pl.multiple_of(i * CHUNK, CHUNK), CHUNK)
-
-    steps = points // CHUNK
-
-    def wait_basis(n):
-        for copy in basis_copies[n]:
-            copy.wait()
-
+    gather(order, raw, x, table, rows_a, rows_b, blocks // 4, blocks // 2)
     wait_basis(0)
-    local = levels[0][2]
-    per_node = steps // local
-    sums = []
-    for node in range(local):
-        def first_step(i, total):
-            return total + dot_nt(x[:, chunk(i)], basis[0, :, chunk(i)])
-
-        sums.append(
-            lax.fori_loop(
-                node * per_node, (node + 1) * per_node, first_step, jnp.zeros((rhs, RANK), F32)
-            )
-        )
+
+    pair = 2 * LANES
+    near = points // 2
+
+    def project(at, total):
+        cols = pl.ds(pl.multiple_of(at, pair), pair)
+        return total + dot_nt(x[:, cols], basis[0, :, cols])
+
+    def beside(i, totals):
+        low, high = totals
+        low = project(i * pair, low)
+        before = near + i * pair - pair
+        cols = pl.ds(pl.multiple_of(before, pair), pair)
+        term = dot_nt(x[:, cols], basis[0, :, cols])
+        return low, high + jnp.where(i > 0, term, 0.0)
+
+    zero = jnp.zeros((rhs, RANK), F32)
+    low, high = gather(
+        order, raw, x, table, rows_a, rows_b, blocks // 2, blocks, beside, (zero, zero)
+    )
+    high = project(points - pair, high)
+    sums = [low, high] if local > 1 else [low + high]
 
     def sweep(n, source, pending):
         ahead = n + 1 < LEVELS
@@ -329,10 +346,10 @@
             pltpu.SemaphoreType.DMA((slots,)),
         ],
         compiler_params=pltpu.CompilerParams(
-            collective_id=0, has_side_effects=True, vmem_limit_bytes=60 * 2**20
+            collective_id=0, has_side_effects=True, vmem_limit_bytes=58 * 2**20
         ),
         cost_estimate=pl.CostEstimate(
-            flops=16 * rhs * RANK * points, bytes_accessed=20 * 2**20, transcendentals=0
+            flops=24 * rhs * RANK * points, bytes_accessed=16 * rhs * points, transcendentals=0
         ),
         name="tree_solve",
     )(right_sides, curve_order, level_bases, capacitance)

time: 36.8 us -> 35.8 us (0.973)
  Pallas kernels: 34.4 us -> 33.4 us
    pallas_call x1, Pallas kernels: 34.4 us -> 33.4 us  [shards(): pl.pallas_call(functools.partial(solve_kernel, levels), out_shape=jax.Sha...]
where the time goes in v6:
time: 35.8 us; the launch traced here: 35.6 us
  Pallas kernels  33.4 us (93%)
  local copies, waits for them, and re-layouts  2.26 us (6%)
    pallas_call x1, Pallas kernels, shards(): pl.pallas_call(functools.partial(solve_kernel, levels), out_shape=jax.Sha...  33.4 us
    unnamed x1, local copies, waits for them, and re-layouts  2.26 us

profile of v6, /device:TPU:0, one launch (start us, length us, event | category | flops | bytes accessed | tf_op | source)
XLA Modules:
  0.0 35.6 jit_solution(16500705658797994209)
XLA Ops:
  0.0 33.4 %tree_solve.1 = bf16[64,8192]{1,0:T(8,128)(2,1)} custom-call(bf16[64,8192]{1,0:T(8,128)(2,1)} %sides.1, s32[1,8192]{1,0:T(1,128)} %order_in.1, bf16[4,64,8192]{2,1,0:T(8,128)(2,1)} %own.1, f32[15,256,256]{2,1,0:T(8,128)} %cap.1), custom_call_target="tpu_custom_call" | custom-call | flops 1610612736 | bytes 8388608 | tf_op jit(solution)/shard_map/tree_solve/pallas_call | solution.py:323
  33.4 2.3 %copy.6 = bf16[64,8192]{1,0:T(8,128)(2,1)} copy(bf16[64,8192]{1,0:T(8,128)(2,1)} %tree_solve.1) | data formatting | bytes 2097152

commit v7 on v6

--- a/solution.py
+++ b/solution.py
@@ -86,8 +86,8 @@
 
 def solve_kernel(
     levels, sides, order_in, own, cap, out,
-    raw, order, x, table, rows_a, rows_b, current, basis, caps, send, recv,
-    in_sems, basis_sems, far_send_sems, far_recv_sems, cap_sems, send_sems, recv_sems,
+    raw, order, x, table, rows_a, rows_b, current, basis, caps, result, send, recv,
+    in_sems, basis_sems, far_send_sems, far_recv_sems, cap_sems, out_sems, send_sems, recv_sems,
 ):
     rhs, points = raw.shape
     half = own.shape[1]
@@ -244,11 +244,10 @@
             copy.wait()
         if local > 1:
             s = jnp.concatenate(sums, axis=1)
-            c = caps[n]
+            c_high, c_low = split(caps[n])
         else:
             total = sums[0]
             sibling = None
-            c = caps[n, 0:RANK, :]
             for at, stage in enumerate(stages):
                 slot0 = stage[0][2]
                 send[slot0] = total.astype(BF16)
@@ -268,6 +267,8 @@
                     products = sweep(n, source, pending)
                     if pending is not None:
                         source = current
+                    c_high, c_low = split(caps[n, 0:RANK, :])
+                    g_high, g_low = split(products[rhs:])
                 for copy, (mask, crosses, slot) in zip(copies, stage):
                     copy.wait()
                     value = recv[slot].astype(F32)
@@ -276,22 +277,27 @@
                     else:
                         total = total + value
             s = jnp.concatenate([total, sibling], axis=1)
-        c_high, c_low = split(c)
         s_high, s_low = split(s)
         coefficients = dot_nt(s_high, c_high) + dot_nt(s_low, c_high) + dot_nt(s_high, c_low)
         coefficients = (coefficients * factor).astype(BF16)
         if local == 1 and not last:
-            g_high, g_low = split(products[rhs:])
             change = jnp.dot(coefficients, g_high, preferred_element_type=F32)
             change = change + jnp.dot(coefficients, g_low, preferred_element_type=F32)
             sums = [products[0:rhs] - change]
             pending = coefficients
             continue
         if local == 1:
+            out_copies = []
             for i in range(steps):
-                here = chunk(i)
+                here = pl.ds(i * CHUNK, CHUNK)
                 update = jnp.dot(coefficients, basis[n, :, here], preferred_element_type=F32)
-                out[:, here] = (source[:, here].astype(F32) - update).astype(BF16)
+                result[:, here] = (source[:, here].astype(F32) - update).astype(BF16)
+                out_copies.append(
+                    pltpu.make_async_copy(result.at[:, here], out.at[:, here], out_sems.at[i])
+                )
+                out_copies[-1].start()
+            for copy in out_copies:
+                copy.wait()
             return
         wait_basis(n + 1)
         next_local = levels[n + 1][2]
@@ -324,7 +330,7 @@
         functools.partial(solve_kernel, levels),
         out_shape=jax.ShapeDtypeStruct((rhs, points), BF16),
         in_specs=[hbm, hbm, hbm, hbm],
-        out_specs=pl.BlockSpec(memory_space=pltpu.VMEM),
+        out_specs=hbm,
         scratch_shapes=[
             pltpu.VMEM((rhs, points), BF16),
             pltpu.SMEM((1, points), jnp.int32),
@@ -335,6 +341,7 @@
             pltpu.VMEM((rhs, points), F32),
             pltpu.VMEM((LEVELS, RANK, points), BF16),
             pltpu.VMEM((LEVELS, 2 * RANK, 2 * RANK), F32),
+            pltpu.VMEM((rhs, points), BF16),
             pltpu.VMEM((slots, rhs, RANK), BF16),
             pltpu.VMEM((slots, rhs, RANK), BF16),
             pltpu.SemaphoreType.DMA((PIECES + 1,)),
@@ -342,6 +349,7 @@
             pltpu.SemaphoreType.DMA((LEVELS,)),
             pltpu.SemaphoreType.DMA((LEVELS,)),
             pltpu.SemaphoreType.DMA((LEVELS, 2)),
+            pltpu.SemaphoreType.DMA((points // CHUNK,)),
             pltpu.SemaphoreType.DMA((slots,)),
             pltpu.SemaphoreType.DMA((slots,)),
         ],

time: 35.8 us -> 35.6 us (level)
  no operation moved by 1% of the time
where the time goes in v7:
time: 35.6 us; the launch traced here: 35.4 us
  Pallas kernels  33.2 us (93%)
  local copies, waits for them, and re-layouts  2.26 us (6%)
    pallas_call x1, Pallas kernels, shards(): pl.pallas_call(functools.partial(solve_kernel, levels), out_shape=jax.Sha...  33.2 us
    unnamed x1, local copies, waits for them, and re-layouts  2.26 us

profile of v7, /device:TPU:0, one launch (start us, length us, event | category | flops | bytes accessed | tf_op | source)
XLA Modules:
  0.0 35.4 jit_solution(5314421902630376574)
XLA Ops:
  0.0 33.2 %tree_solve.1 = bf16[64,8192]{1,0:T(8,128)(2,1)} custom-call(bf16[64,8192]{1,0:T(8,128)(2,1)} %sides.1, s32[1,8192]{1,0:T(1,128)} %order_in.1, bf16[4,64,8192]{2,1,0:T(8,128)(2,1)} %own.1, f32[15,256,256]{2,1,0:T(8,128)} %cap.1), custom_call_target="tpu_custom_call" | custom-call | flops 1610612736 | bytes 8388608 | tf_op jit(solution)/shard_map/tree_solve/pallas_call | solution.py:329
  33.2 2.3 %copy.6 = bf16[64,8192]{1,0:T(8,128)(2,1)} copy(bf16[64,8192]{1,0:T(8,128)(2,1)} %tree_solve.1) | data formatting | bytes 2097152

commit v8 on v7

--- a/solution.py
+++ b/solution.py
@@ -11,7 +11,7 @@
 RANK = 128
 LEVELS = 4
 LANES = 128
-CHUNK = 1024
+CHUNK = 2048
 PIECES = 4
 STAGE_BITS = 2
 MESH = pl.DeviceIdType.MESH

time: 35.6 us -> 34.7 us (0.975)
  Pallas kernels: 33.2 us -> 32.3 us
    pallas_call x1, Pallas kernels: 33.2 us -> 32.3 us  [shards(): pl.pallas_call(functools.partial(solve_kernel, levels), out_shape=jax.Sha...]
where the time goes in v8:
time: 34.7 us; the launch traced here: 34.5 us
  Pallas kernels  32.3 us (93%)
  local copies, waits for them, and re-layouts  2.26 us (7%)
    pallas_call x1, Pallas kernels, shards(): pl.pallas_call(functools.partial(solve_kernel, levels), out_shape=jax.Sha...  32.3 us
    unnamed x1, local copies, waits for them, and re-layouts  2.26 us

profile of v8, /device:TPU:0, one launch (start us, length us, event | category | flops | bytes accessed | tf_op | source)
XLA Modules:
  0.0 34.5 jit_solution(13788067896848031059)
XLA Ops:
  0.0 32.3 %tree_solve.1 = bf16[64,8192]{1,0:T(8,128)(2,1)} custom-call(bf16[64,8192]{1,0:T(8,128)(2,1)} %sides.1, s32[1,8192]{1,0:T(1,128)} %order_in.1, bf16[4,64,8192]{2,1,0:T(8,128)(2,1)} %own.1, f32[15,256,256]{2,1,0:T(8,128)} %cap.1), custom_call_target="tpu_custom_call" | custom-call | flops 1610612736 | bytes 8388608 | tf_op jit(solution)/shard_map/tree_solve/pallas_call | solution.py:329
  32.3 2.3 %copy.6 = bf16[64,8192]{1,0:T(8,128)(2,1)} copy(bf16[64,8192]{1,0:T(8,128)(2,1)} %tree_solve.1) | data formatting | bytes 2097152
